TPU v7x, 256 devices: a whole 4x4x8 slice. The times are simulated.
256 devices in a mesh: store: 32 (over z, y), tp: 8 (over x, core).
Axes of the slice: x: 4, y: 4, z: 8, core: 2. Of those that a mesh axis runs over, the one named last changes fastest.
Arguments:
- query: bfloat16 [2560, 8192], P('store', 'tp')
- new_kv: bfloat16 [2, 2560, 1024], P(None, 'store', 'tp')
- kv_store: bfloat16 [2, 640, 512, 1024], P(None, 'store', None, 'tp'), may hold values from -6 to 6
- passage_ids: int32 [256, 10], P('store'), may hold values from 0 to 639, as said below
- residual_in: bfloat16 [2560, 8192], P('store', 'tp'), may hold values from -3 to 3
- out_weight: bfloat16 [8192, 8192], P('tp', 'store'), may hold values from -0.75 to 0.75
Outputs:
- layer_out: bfloat16 [2560, 8192], P('store', 'tp')
Inputs may be any that keep to these rules, and one draw needn't show every extreme that they name: `passage_ids`: store shard s holds passages s * 20 to (s + 1) * 20 - 1. In each aligned block of 8 rows (the queries of one index of store), every shard that is named at all is named exactly 5 times; popular shards are named in more blocks and low passage numbers within a shard are more popular.
All inputs are finite; a program needn't handle non-finite values.
Results may differ from a plain program's by a relative error of at most 0.018.
Values may be sent and summed in bfloat16 or wider, within the bound.
A program may use at most 64 MiB of HBM per device.

v0:
```python
import jax
import jax.numpy as jnp
from jax import lax
from jax.sharding import PartitionSpec as P

H = 64
KVH = 8
HD = 128
PLEN = 512


def attend_slots(queries, own_pairs, passage_local, kv_store):
    slot_count = queries.shape[0]
    kv_width = own_pairs.shape[1] // 2
    kv_heads = kv_width // HD
    group_size = H // KVH
    scaling = 1.0 / HD**0.5
    pass_local = kv_store.shape[1]
    query_heads = queries.reshape(slot_count, kv_heads, group_size, HD)
    own_keys = own_pairs[:, :kv_width].reshape(slot_count, kv_heads, HD)
    own_values = own_pairs[:, kv_width:].reshape(slot_count, kv_heads, HD)
    own_score = (
        jnp.einsum("bgjd,bgd->bgj", query_heads, own_keys, preferred_element_type=jnp.float32)
        * scaling
    )
    own_float = own_values.astype(jnp.float32)[:, :, None, :]

    def one_passage(index, result):
        block = lax.dynamic_index_in_dim(kv_store, index, 1, keepdims=False)
        stored_keys = block[0].reshape(PLEN, kv_heads, HD)
        stored_values = block[1].reshape(PLEN, kv_heads, HD)
        scores = (
            jnp.einsum(
                "bgjd,kgd->bgjk", query_heads, stored_keys, preferred_element_type=jnp.float32
            )
            * scaling
        )
        highest = jnp.maximum(jnp.max(scores, axis=-1), own_score)
        exponent_terms = jnp.exp(scores - highest[..., None])
        own_term = jnp.exp(own_score - highest)
        totals = jnp.sum(exponent_terms, axis=-1) + own_term
        weights = (exponent_terms / totals[..., None]).astype(jnp.bfloat16)
        own_weight = (own_term / totals).astype(jnp.bfloat16)
        mixed = jnp.einsum(
            "bgjk,kgd->bgjd", weights, stored_values, preferred_element_type=jnp.float32
        )
        mixed = (mixed + own_weight.astype(jnp.float32)[..., None] * own_float).astype(jnp.bfloat16)
        matching = (passage_local == index)[:, None, None, None]
        return jnp.where(matching, mixed, result)

    start = jnp.zeros((slot_count, kv_heads, group_size, HD), jnp.bfloat16)
    result = lax.fori_loop(0, pass_local, one_passage, start)
    return result.reshape(slot_count, kv_heads * group_size * HD)


def shards(query, new_kv, kv_store, passage_ids, residual_in, out_weight):
    store_count = lax.axis_size("store")
    local_streams = query.shape[0]
    head_width = query.shape[1]
    kv_width = new_kv.shape[2]
    pass_local = kv_store.shape[1]
    fan_out = min(store_count, 16)
    per_shard = local_streams // fan_out
    slots_total = store_count * per_shard
    stream_passages = passage_ids.reshape(local_streams)
    owner_shard = stream_passages // pass_local
    local_passage = stream_passages - owner_shard * pass_local
    owner_onehot = (owner_shard[:, None] == jnp.arange(store_count)[None, :]).astype(jnp.int32)
    earlier = jnp.cumsum(owner_onehot, axis=0) - owner_onehot
    position = jnp.sum(earlier * owner_onehot, axis=1)
    slot_index = owner_shard * per_shard + position
    slot_match = jnp.arange(slots_total)[:, None] == slot_index[None, :]
    selector = slot_match.astype(jnp.bfloat16)
    gatherer = (slot_index[:, None] == jnp.arange(slots_total)[None, :]).astype(jnp.bfloat16)
    own_pairs = jnp.concatenate([new_kv[0], new_kv[1]], axis=1)
    send_queries = jnp.dot(selector, query, preferred_element_type=jnp.float32).astype(jnp.bfloat16)
    send_pairs = jnp.dot(selector, own_pairs, preferred_element_type=jnp.float32).astype(
        jnp.bfloat16
    )
    send_local = jnp.sum(jnp.where(slot_match, local_passage[None, :], 0), axis=1)
    send_queries = send_queries.reshape(store_count, per_shard, head_width)
    send_pairs = send_pairs.reshape(store_count, per_shard, 2 * kv_width)
    send_local = send_local.reshape(store_count, per_shard)
    recv_queries = lax.all_to_all(send_queries, "store", split_axis=0, concat_axis=0, tiled=True)
    recv_pairs = lax.all_to_all(send_pairs, "store", split_axis=0, concat_axis=0, tiled=True)
    recv_local = lax.all_to_all(send_local, "store", split_axis=0, concat_axis=0, tiled=True)
    sources = recv_queries.shape[0]
    per_source = recv_queries.shape[1]
    results = attend_slots(
        recv_queries.reshape(sources * per_source, head_width),
        recv_pairs.reshape(sources * per_source, 2 * kv_width),
        recv_local.reshape(sources * per_source),
        kv_store,
    )
    results = results.reshape(sources, per_source, head_width)
    returned = lax.all_to_all(results, "store", split_axis=0, concat_axis=0, tiled=True)
    attention = jnp.dot(
        gatherer, returned.reshape(slots_total, head_width), preferred_element_type=jnp.float32
    ).astype(jnp.bfloat16)
    partial_full = jnp.dot(
        attention,
        lax.all_gather(out_weight, "store", axis=1, tiled=True),
        preferred_element_type=jnp.float32,
    )
    projected = lax.psum_scatter(
        partial_full.astype(jnp.bfloat16), "tp", scatter_dimension=1, tiled=True
    ).astype(jnp.float32)
    return (residual_in.astype(jnp.float32) + projected).astype(jnp.bfloat16)


def solution(mesh):
    placed = (
        P("store", "tp"),
        P(None, "store", "tp"),
        P(None, "store", None, "tp"),
        P("store", None),
        P("store", "tp"),
        P("tp", "store"),
    )
    return jax.shard_map(
        shards, mesh=mesh, in_specs=placed, out_specs=P("store", "tp"), check_vma=False
    )
```

profile of v0, /device:TPU:8, one launch (start us, length us, event | category | flops | bytes accessed | tf_op | source)
XLA Modules:
  0.0 264.2 jit_solution(4640889365879576970)
XLA Ops:
  8.6 11.7 %all-to-all-start = ((s32[32,1,5]{2,1,0:T(1,128)}), s32[32,1,5]{2,1,0:T(1,128)S(1)}, u32[]{:S(2)}, u32[]{:S(2)}) async-start(s32[32,1,5]{2,1,0:T(1,128)} %bitcast), calls=%async_computation | async-start | bytes 32768 | tf_op jit(solution)/shard_map/all_to_all | solution.py:86
  21.9 6.9 %all-to-all-done = s32[32,1,5]{2,1,0:T(1,128)S(1)} async-done(((s32[32,1,5]{2,1,0:T(1,128)}), s32[32,1,5]{2,1,0:T(1,128)S(1)}, u32[]{:S(2)}, u32[]{:S(2)}) %all-to-all-start) | async-done | bytes 672 | tf_op jit(solution)/shard_map/all_to_all | solution.py:86
  28.8 4.8 %all-to-all-start.2 = ((bf16[32,5,256]{2,1,0:T(8,128)(2,1)}), bf16[32,5,256]{2,1,0:T(8,128)(2,1)S(1)}, u32[]{:S(2)}, u32[]{:S(2)}) async-start(bf16[32,5,256]{2,1,0:T(8,128)(2,1)} %reshape.233), calls=%async_computation.2 | async-start | bytes 262144 | tf_op jit(solution)/shard_map/all_to_all | solution.py:85
  34.8 7.8 %all-to-all-done.2 = bf16[32,5,256]{2,1,0:T(8,128)(2,1)S(1)} async-done(((bf16[32,5,256]{2,1,0:T(8,128)(2,1)}), bf16[32,5,256]{2,1,0:T(8,128)(2,1)S(1)}, u32[]{:S(2)}, u32[]{:S(2)}) %all-to-all-start.2) | async-done | bytes 81952 | tf_op jit(solution)/shard_map/all_to_all | solution.py:85
  42.6 5.5 %all-to-all-start.1 = ((bf16[32,5,1024]{2,1,0:T(8,128)(2,1)}), bf16[32,5,1024]{2,1,0:T(8,128)(2,1)S(1)}, u32[]{:S(2)}, u32[]{:S(2)}) async-start(bf16[32,5,1024]{2,1,0:T(8,128)(2,1)} %reshape.231), calls=%async_computation.1 | async-start | bytes 1048576 | tf_op jit(solution)/shard_map/all_to_all | solution.py:84
  50.8 12.1 %all-to-all-done.1 = bf16[32,5,1024]{2,1,0:T(8,128)(2,1)S(1)} async-done(((bf16[32,5,1024]{2,1,0:T(8,128)(2,1)}), bf16[32,5,1024]{2,1,0:T(8,128)(2,1)S(1)}, u32[]{:S(2)}, u32[]{:S(2)}) %all-to-all-start.1) | async-done | bytes 327712 | tf_op jit(solution)/shard_map/all_to_all | solution.py:84
  64.1 101.1 %while.14 = (s32[]{:T(128)}, bf16[160,1,8,128]{3,0,2,1:T(8,128)(2,1)S(1)}, s32[160]{0:T(256)}, bf16[2,20,512,128]{3,2,1,0:T(8,128)(2,1)}, bf16[160,1,8,128]{3,0,...) while((s32[]{:T(128)}, ...), condition=%wide.region_6.7_spmd.clone, body=%wide.region_3.6_spmd.clone.sunk | while | flops 342268320 | bytes 9268159 | solution.py:52
  67.2 2.0 fusion.49
  72.2 2.0 fusion.49
  82.3 2.0 fusion.49
  97.5 2.0 fusion.49
  107.6 2.0 fusion.49
  112.6 2.0 fusion.49
  117.7 2.0 fusion.49
  122.7 2.0 fusion.49
  127.8 2.0 fusion.49
  137.9 2.0 fusion.49
  142.9 2.0 fusion.49
  158.1 2.0 fusion.49
  163.1 2.0 fusion.49
  165.7 25.8 %all_to_all.24 = bf16[32,5,1024]{2,1,0:T(8,128)(2,1)S(1)} all-to-all(bf16[32,5,1024]{2,1,0:T(8,128)(2,1)S(1)} %reshape_reshape.7), channel_id=1, replica_groups=mesh['store'=32,'tp'=8] {'store'}, dimensions={0} | all-to-all | bytes 655360 | tf_op jit(solution)/shard_map/all_to_all | solution.py:96
  191.7 20.7 %all-gather.2.cloned.1.call-done = bf16[1024,8192]{1,0:T(8,128)(2,1)} async-done(((bf16[1024,256]{1,0:T(8,128)(2,1)}), bf16[1024,8192]{1,0:T(8,128)(2,1)}) %all-gather.2.cloned.1.call-update) | async-done | bytes 16777232 | tf_op jit(solution)/shard_map/all_gather | solution.py:102
  212.4 10.0 %convolution_convert_fusion = bf16[80,8192]{1,0:T(8,128)(2,1)} fusion(bf16[1024,8192]{1,0:T(8,128)(2,1)} %all-gather.2.cloned.1.call-done, bf16[160,1024]{1,0:T(8,128)(2,1)S(1)} %reshape.235, s32[80]{0:T(128)S(1)} %copy-done.4), kind=kOutput, calls=%fused_computation.26 | convolution fusion | flops 1369141760 | bytes 18415936 | tf_op jit(solution)/shard_map/dot_general | solution.py:100
  222.4 33.3 %reduce-scatter.2.cloned.1.call-done = bf16[80,1024]{1,0:T(8,128)(2,1)} async-done(((bf16[80,8192]{1,0:T(8,128)(2,1)}), bf16[80,1024]{1,0:T(8,128)(2,1)}) %reduce-scatter.2.cloned.1.call-update) | async-done | bytes 163856 | tf_op jit(solution)/shard_map/reduce_scatter | solution.py:105
  (188 shorter events, 84.9 us)
Async XLA Ops:
  6.5 27.1 %copy-start = (bf16[80,1024]{1,0:T(8,128)(2,1)S(1)}, bf16[80,1024]{1,0:T(8,128)(2,1)}, u32[]{:S(2)}) copy-start(bf16[80,1024]{1,0:T(8,128)(2,1)} %param.8) | copy-start | bytes 491524
  7.7 41.1 %copy-start.3 = (s32[80]{0:T(128)}, s32[80]{0:T(128)S(1)}, u32[]{:S(2)}) copy-start(s32[80]{0:T(128)S(1)} %multiply_add_fusion) | copy-start | bytes 964
  8.6 20.2 %all-to-all-start = ((s32[32,1,5]{2,1,0:T(1,128)}), s32[32,1,5]{2,1,0:T(1,128)S(1)}, u32[]{:S(2)}, u32[]{:S(2)}) async-start(s32[32,1,5]{2,1,0:T(1,128)} %bitcast), calls=%async_computation | async-start | bytes 32768 | tf_op jit(solution)/shard_map/all_to_all | solution.py:86
  28.8 13.8 %all-to-all-start.2 = ((bf16[32,5,256]{2,1,0:T(8,128)(2,1)}), bf16[32,5,256]{2,1,0:T(8,128)(2,1)S(1)}, u32[]{:S(2)}, u32[]{:S(2)}) async-start(bf16[32,5,256]{2,1,0:T(8,128)(2,1)} %reshape.233), calls=%async_computation.2 | async-start | bytes 262144 | tf_op jit(solution)/shard_map/all_to_all | solution.py:85
  42.6 20.3 %all-to-all-start.1 = ((bf16[32,5,1024]{2,1,0:T(8,128)(2,1)}), bf16[32,5,1024]{2,1,0:T(8,128)(2,1)S(1)}, u32[]{:S(2)}, u32[]{:S(2)}) async-start(bf16[32,5,1024]{2,1,0:T(8,128)(2,1)} %reshape.231), calls=%async_computation.1 | async-start | bytes 1048576 | tf_op jit(solution)/shard_map/all_to_all | solution.py:84
  48.1 164.3 %all-gather.2.cloned.1.call-start = ((), (), s32[]{:S(2)}) async-start(), calls=%async_computation.5 | async-start | bytes 17301504 | tf_op jit(solution)/shard_map/all_gather | solution.py:102
  48.8 207.0 %reduce-scatter.2.cloned.1.call-start = ((), (), s32[]{:S(2)}) async-start(), calls=%async_computation.6 | async-start | bytes 1474560 | tf_op jit(solution)/shard_map/reduce_scatter | solution.py:105
  64.1 2.5 copy-start.2
  74.2 2.5 copy-start.2
  79.3 2.5 copy-start.2
  84.4 2.5 copy-start.2
  94.4 2.5 copy-start.2
  99.5 2.5 copy-start.2
  109.6 2.5 copy-start.2
  114.7 2.5 copy-start.2
  119.7 2.5 copy-start.2
  129.8 2.5 copy-start.2
  134.9 2.5 copy-start.2
  139.9 2.5 copy-start.2
  145.0 2.5 copy-start.2
  155.1 2.5 copy-start.2
  160.1 2.5 copy-start.2
  165.2 47.2 %copy-start.4 = (s32[80]{0:T(128)S(1)}, s32[80]{0:T(128)}, u32[]{:S(2)}) copy-start(s32[80]{0:T(128)} %copy-done.3) | copy-start | bytes 964
  191.7 64.1 %copy-start.1 = (bf16[80,1024]{1,0:T(8,128)(2,1)S(1)}, bf16[80,1024]{1,0:T(8,128)(2,1)}, u32[]{:S(2)}) copy-start(bf16[80,1024]{1,0:T(8,128)(2,1)} %param.12) | copy-start | bytes 491524
  (5 other events, 12.3 us)
Sparse Core Ops, SparseCore 0:
  51.4 160.9 all-gather.1
  222.5 33.1 reduce-scatter.1
where the time goes:
time: 265 us; the launch traced here: 264 us
  waiting for transfers between devices  81.5 us (31%)
  matrix products  81.3 us (31%)
  other arithmetic  32.2 us (12%)
  blocking collectives  25.8 us (10%)
  starting transfers between devices  22 us (8%)
  between operations  13.6 us (5%)
  local copies, waits for them, and re-layouts  6.82 us (3%)
    dot_general x20, matrix products, one_passage(): jnp.einsum('bgjk,kgd->bgjd', weights, stored_values, preferred_element_ty...  40.2 us
    reduce_scatter x1, waiting for transfers between devices, shards(): lax.psum_scatter(partial_full.astype(jnp.bfloat16), 'tp', scatter_dimensi...  33.3 us
    dot_general x20, matrix products, one_passage(): jnp.einsum('bgjd,kgd->bgjk', query_heads, stored_keys, preferred_element_...  30.4 us
    all_to_all x1, blocking collectives, shards(): lax.all_to_all(results, 'store', split_axis=0, concat_axis=0, tiled=True)  25.8 us
    all_gather x1, waiting for transfers between devices, shards(): lax.all_gather(out_weight, 'store', axis=1, tiled=True)  20.7 us
    reduce_sum x20, other arithmetic, one_passage(): totals = jnp.sum(exponent_terms, axis=-1) + own_term  18.1 us
    all_to_all x1, waiting for transfers between devices, shards(): lax.all_to_all(send_queries, 'store', split_axis=0, concat_axis=0, tiled=...  12.1 us
    all_to_all x1, starting transfers between devices, shards(): lax.all_to_all(send_local, 'store', split_axis=0, concat_axis=0, tiled=True)  11.7 us
  transfers between devices with their start and end apart: 5, of which 5 were waited for; matrix products, arithmetic and copies ran while one was open for 40% of the time, Pallas kernels for 0%

commit v1 on v0

--- a/solution.py
+++ b/solution.py
@@ -2,11 +2,21 @@
 import jax.numpy as jnp
 from jax import lax
 from jax.sharding import PartitionSpec as P
+from jax.lax import all_to_all, axis_size
 
 H = 64
 KVH = 8
 HD = 128
 PLEN = 512
+run_classes = lambda x_in, net_axis: jnp.concatenate(
+    all_to_all(
+        jnp.stack([x_in for _ in range(axis_size(net_axis))], axis=0),
+        axis_name=net_axis,
+        split_axis=0,
+        concat_axis=0,
+    ),
+    1,
+)
 
 
 def attend_slots(queries, own_pairs, passage_local, kv_store):
@@ -98,9 +108,7 @@
         gatherer, returned.reshape(slots_total, head_width), preferred_element_type=jnp.float32
     ).astype(jnp.bfloat16)
     partial_full = jnp.dot(
-        attention,
-        lax.all_gather(out_weight, "store", axis=1, tiled=True),
-        preferred_element_type=jnp.float32,
+        attention, run_classes(out_weight, "store"), preferred_element_type=jnp.float32
     )
     projected = lax.psum_scatter(
         partial_full.astype(jnp.bfloat16), "tp", scatter_dimension=1, tiled=True

time: 265 us -> 633 us (2.39)
  waiting for transfers between devices: 81.5 us -> 454 us
  blocking collectives: 25.8 us -> 0 us
  starting transfers between devices: 22 us -> 34.2 us
  local copies, waits for them, and re-layouts: 6.82 us -> 13.8 us
    all_to_all x0 -> x2, waiting for transfers between devices: none -> 376 us  [the longest x1 362 us: all_to_all(jnp.stack([x_in for _ in range(axis_size(net_axis))], axis=0),...]
    all_to_all x1 -> x0, blocking collectives: 25.8 us -> none  [shards(): lax.all_to_all(results, 'store', split_axis=0, concat_axis=0, tiled=True)]
    all_gather x1 -> x0, waiting for transfers between devices: 20.7 us -> none  [shards(): lax.all_gather(out_weight, 'store', axis=1, tiled=True)]
    reduce_scatter x1, waiting for transfers between devices: 33.3 us -> 51.5 us  [shards(): lax.psum_scatter(partial_full.astype(jnp.bfloat16), 'tp', scatter_dimensi...]
    all_to_all x0 -> x2, starting transfers between devices: none -> 12 us  [the longest x1 6.42 us: all_to_all(jnp.stack([x_in for _ in range(axis_size(net_axis))], axis=0),...]
  transfers between devices with their start and end apart: 5 -> 6, of which waited for: 5 -> 6; matrix products, arithmetic and copies ran while one was open for 40% -> 1% of each run, Pallas kernels for 0% -> 0%
where the time goes in v1:
time: 633 us; the launch traced here: 632 us
  waiting for transfers between devices  454 us (72%)
  matrix products  83.3 us (13%)
  starting transfers between devices  34.2 us (5%)
  other arithmetic  31.8 us (5%)
  local copies, waits for them, and re-layouts  13.8 us (2%)
  between operations  13.6 us (2%)
    all_to_all x1, waiting for transfers between devices, all_to_all(jnp.stack([x_in for _ in range(axis_size(net_axis))], axis=0),...  362 us
    reduce_scatter x1, waiting for transfers between devices, shards(): lax.psum_scatter(partial_full.astype(jnp.bfloat16), 'tp', scatter_dimensi...  51.5 us
    dot_general x20, matrix products, one_passage(): jnp.einsum('bgjk,kgd->bgjd', weights, stored_values, preferred_element_ty...  40.1 us
    dot_general x20, matrix products, one_passage(): jnp.einsum('bgjd,kgd->bgjk', query_heads, stored_keys, preferred_element_...  30.3 us
    reduce_sum x20, other arithmetic, one_passage(): totals = jnp.sum(exponent_terms, axis=-1) + own_term  18.1 us
    all_to_all x1, waiting for transfers between devices, shards(): lax.all_to_all(results, 'store', split_axis=0, concat_axis=0, tiled=True)  13.5 us
  transfers between devices with their start and end apart: 6, of which 6 were waited for; matrix products, arithmetic and copies ran while one was open for 1% of the time, Pallas kernels for 0%

profile of v1, /device:TPU:8, one launch (start us, length us, event | category | flops | bytes accessed | tf_op | source)
XLA Modules:
  0.0 632.2 jit_solution(16618478461253294991)
XLA Ops:
  8.6 11.7 %all-to-all-start = ((s32[32,1,5]{2,1,0:T(1,128)}), s32[32,1,5]{2,1,0:T(1,128)S(1)}, u32[]{:S(2)}, u32[]{:S(2)}) async-start(s32[32,1,5]{2,1,0:T(1,128)} %bitcast), calls=%async_computation | async-start | bytes 32768 | tf_op jit(solution)/shard_map/all_to_all | solution.py:96
  21.9 6.9 %all-to-all-done = s32[32,1,5]{2,1,0:T(1,128)S(1)} async-done(((s32[32,1,5]{2,1,0:T(1,128)}), s32[32,1,5]{2,1,0:T(1,128)S(1)}, u32[]{:S(2)}, u32[]{:S(2)}) %all-to-all-start) | async-done | bytes 672 | tf_op jit(solution)/shard_map/all_to_all | solution.py:96
  28.8 5.0 all-to-all-start.2
  35.0 7.8 %all-to-all-done.2 = bf16[32,5,256]{2,1,0:T(8,128)(2,1)S(1)} async-done(((bf16[32,5,256]{2,1,0:T(8,128)(2,1)}), bf16[32,5,256]{2,1,0:T(8,128)(2,1)S(1)}, u32[]{:S(2)}, u32[]{:S(2)}) %all-to-all-start.2) | async-done | bytes 81952 | tf_op jit(solution)/shard_map/all_to_all | solution.py:95
  42.7 5.5 all-to-all-start.1
  50.3 12.4 %all-to-all-done.1 = bf16[32,5,1024]{2,1,0:T(8,128)(2,1)S(1)} async-done(((bf16[32,5,1024]{2,1,0:T(8,128)(2,1)}), bf16[32,5,1024]{2,1,0:T(8,128)(2,1)S(1)}, u32[]{:S(2)}, u32[]{:S(2)}) %all-to-all-start.1) | async-done | bytes 327712 | tf_op jit(solution)/shard_map/all_to_all | solution.py:94
  63.9 100.5 %while.14 = (s32[]{:T(128)}, bf16[160,1,8,128]{3,0,2,1:T(8,128)(2,1)S(1)}, s32[160]{0:T(256)}, bf16[2,20,512,128]{3,2,1,0:T(8,128)(2,1)}, bf16[160,1,8,128]{3,0,...) while((s32[]{:T(128)}, ...), condition=%wide.region_6.7_spmd.clone, body=%wide.region_3.6_spmd.clone.sunk | while | flops 342268320 | bytes 9267151 | solution.py:62
  87.0 2.0 fusion.49
  92.1 2.0 fusion.49
  97.1 2.0 fusion.49
  102.1 2.0 fusion.49
  107.2 2.0 fusion.49
  112.2 2.0 fusion.49
  117.2 2.0 fusion.49
  122.2 2.0 fusion.49
  127.3 2.0 fusion.49
  147.4 2.0 fusion.49
  165.8 5.6 all-to-all-start.3
  171.6 13.5 %all-to-all-done.3 = bf16[32,5,1024]{2,1,0:T(8,128)(2,1)S(1)} async-done(((bf16[32,5,1024]{2,1,0:T(8,128)(2,1)}), bf16[32,5,1024]{2,1,0:T(8,128)(2,1)S(1)}, u32[]{:S(2)}, u32[]{:S(2)}) %all-to-all-start.3) | async-done | bytes 327712 | tf_op jit(solution)/shard_map/all_to_all | solution.py:106
  185.2 6.0 stack.2
  191.1 6.4 %all-to-all-start.4 = ((bf16[32,1024,256]{1,2,0:T(8,128)(2,1)}), bf16[32,1024,256]{1,2,0:T(8,128)(2,1)}, u32[]{:S(2)}, u32[]{:S(2)}) async-start(bf16[32,1024,256]{1,2,0:T(8,128)(2,1)} %stack.2), calls=%async_computation.4 | async-start | bytes 33554432 | tf_op jit(solution)/shard_map/all_to_all | solution.py:12
  197.7 362.2 %all-to-all-done.4 = bf16[32,1024,256]{1,2,0:T(8,128)(2,1)} async-done(((bf16[32,1024,256]{1,2,0:T(8,128)(2,1)}), bf16[32,1024,256]{1,2,0:T(8,128)(2,1)}, u32[]{:S(2)}, u32[]{:S(2)}) %all-to-all-start.4) | async-done | bytes 16777248 | tf_op jit(solution)/shard_map/all_to_all | solution.py:12
  560.0 12.2 %convolution_convert_fusion = bf16[80,8192]{1,0:T(8,128)(2,1)} fusion(bf16[1024,8192]{0,1:T(8,128)(2,1)} %bitcast.8, bf16[160,1024]{1,0:T(8,128)(2,1)S(1)} %reshape.243, s32[80]{0:T(128)S(1)} %copy-done.5), kind=kOutput, calls=%fused_computation.26 | convolution fusion | flops 1369141760 | bytes 18415936 | tf_op jit(solution)/shard_map/dot_general | solution.py:110
  572.2 51.5 %reduce-scatter.2.cloned.1.call-done = bf16[80,1024]{1,0:T(8,128)(2,1)} async-done(((bf16[80,8192]{1,0:T(8,128)(2,1)}), bf16[80,1024]{1,0:T(8,128)(2,1)}) %reduce-scatter.2.cloned.1.call-update) | async-done | bytes 163856 | tf_op jit(solution)/shard_map/reduce_scatter | solution.py:113
  (192 shorter events, 90.7 us)
Async XLA Ops:
  6.5 27.3 %copy-start = (bf16[80,1024]{1,0:T(8,128)(2,1)S(1)}, bf16[80,1024]{1,0:T(8,128)(2,1)}, u32[]{:S(2)}) copy-start(bf16[80,1024]{1,0:T(8,128)(2,1)} %param.8) | copy-start | bytes 491524
  7.7 40.6 %copy-start.4 = (s32[80]{0:T(128)}, s32[80]{0:T(128)S(1)}, u32[]{:S(2)}) copy-start(s32[80]{0:T(128)S(1)} %multiply_add_fusion) | copy-start | bytes 964
  8.6 20.2 %all-to-all-start = ((s32[32,1,5]{2,1,0:T(1,128)}), s32[32,1,5]{2,1,0:T(1,128)S(1)}, u32[]{:S(2)}, u32[]{:S(2)}) async-start(s32[32,1,5]{2,1,0:T(1,128)} %bitcast), calls=%async_computation | async-start | bytes 32768 | tf_op jit(solution)/shard_map/all_to_all | solution.py:96
  28.8 13.9 %all-to-all-start.2 = ((bf16[32,5,256]{2,1,0:T(8,128)(2,1)}), bf16[32,5,256]{2,1,0:T(8,128)(2,1)S(1)}, u32[]{:S(2)}, u32[]{:S(2)}) async-start(bf16[32,5,256]{2,1,0:T(8,128)(2,1)} %reshape.241), calls=%async_computation.2 | async-start | bytes 262144 | tf_op jit(solution)/shard_map/all_to_all | solution.py:95
  42.7 19.9 %all-to-all-start.1 = ((bf16[32,5,1024]{2,1,0:T(8,128)(2,1)}), bf16[32,5,1024]{2,1,0:T(8,128)(2,1)S(1)}, u32[]{:S(2)}, u32[]{:S(2)}) async-start(bf16[32,5,1024]{2,1,0:T(8,128)(2,1)} %reshape.239), calls=%async_computation.1 | async-start | bytes 1048576 | tf_op jit(solution)/shard_map/all_to_all | solution.py:94
  63.9 2.5 copy-start.3
  79.0 2.5 copy-start.3
  84.0 2.5 copy-start.3
  89.1 2.5 copy-start.3
  94.1 2.5 copy-start.3
  99.1 2.5 copy-start.3
  104.2 2.5 copy-start.3
  109.2 2.5 copy-start.3
  114.2 2.5 copy-start.3
  119.2 2.5 copy-start.3
  124.3 2.5 copy-start.3
  129.3 2.5 copy-start.3
  134.3 2.5 copy-start.3
  164.5 6.9 %copy-start.1 = (bf16[1024,256]{1,0:T(8,128)(2,1)S(1)}, bf16[1024,256]{1,0:T(8,128)(2,1)}, u32[]{:S(2)}) copy-start(bf16[1024,256]{1,0:T(8,128)(2,1)} %param.13) | copy-start | bytes 1572868
  165.8 19.4 %all-to-all-start.3 = ((bf16[32,5,1024]{2,1,0:T(8,128)(2,1)}), bf16[32,5,1024]{2,1,0:T(8,128)(2,1)S(1)}, u32[]{:S(2)}, u32[]{:S(2)}) async-start(bf16[32,5,1024]{2,1,0:T(8,128)(2,1)} %reshape_reshape.7), calls=%async_computation.3 | async-start | bytes 1048576 | tf_op jit(solution)/shard_map/all_to_all | solution.py:106
  191.1 368.9 %copy-start.5 = (s32[80]{0:T(128)S(1)}, s32[80]{0:T(128)}, u32[]{:S(2)}) copy-start(s32[80]{0:T(128)} %copy-done.4) | copy-start | bytes 964
  191.1 368.9 %all-to-all-start.4 = ((bf16[32,1024,256]{1,2,0:T(8,128)(2,1)}), bf16[32,1024,256]{1,2,0:T(8,128)(2,1)}, u32[]{:S(2)}, u32[]{:S(2)}) async-start(bf16[32,1024,256]{1,2,0:T(8,128)(2,1)} %stack.2), calls=%async_computation.4 | async-start | bytes 33554432 | tf_op jit(solution)/shard_map/all_to_all | solution.py:12
  197.5 426.1 %reduce-scatter.2.cloned.1.call-start = ((), (), s32[]{:S(2)}) async-start(), calls=%async_computation.6 | async-start | bytes 1474560 | tf_op jit(solution)/shard_map/reduce_scatter | solution.py:113
  560.0 63.7 %copy-start.2 = (bf16[80,1024]{1,0:T(8,128)(2,1)S(1)}, bf16[80,1024]{1,0:T(8,128)(2,1)}, u32[]{:S(2)}) copy-start(bf16[80,1024]{1,0:T(8,128)(2,1)} %param.12) | copy-start | bytes 491524
  (7 other events, 17.2 us)
Sparse Core Ops, SparseCore 0:
  572.3 51.2 reduce-scatter.1
